TPU v7x, 512 devices: a whole 4x4x16 slice. The times are simulated.
512 devices in a mesh: pipe: 16 (over z), seq: 32 (over x, y, core).
Axes of the slice: x: 4, y: 4, z: 16, core: 2. Of those that a mesh axis runs over, the one named last changes fastest.
Arguments:
- handoff: bfloat16 [16, 4096, 512], P('pipe', 'seq'), may hold values from -6 to 6
- gate_input: bfloat16 [16, 4096, 512], P('pipe', 'seq'), may hold values from -6 to 6
- source: bfloat16 [16, 4096, 512], P('pipe', 'seq'), may hold values from -6 to 6
- long_filter: bfloat16 [16, 4096, 512], P('pipe', 'seq'), may hold values from -6 to 6
- decay_rates: float32 [16, 512], P('pipe'), may hold values from 6.1035156e-05 to 0.0014648438
Outputs:
- grad_gate: bfloat16 [16, 4096, 512], P('pipe', 'seq')
- grad_source: bfloat16 [16, 4096, 512], P('pipe', 'seq')
- grad_filter: float32 [16, 4096, 512], P('pipe', 'seq')
All inputs are finite; a program needn't handle non-finite values.
Results may differ from a plain program's by a relative error of at most 0.0049.
Values may be sent and summed in bfloat16 or wider, within the bound.
A program may use at most 64 MiB of HBM per device.

v0:
```python
import functools

import jax
import jax.numpy as jnp
import ml_dtypes
import numpy as np
from jax import lax
from jax.experimental import pallas as pl
from jax.experimental.pallas import tpu as pltpu
from jax.sharding import PartitionSpec as P

MESH = pl.DeviceIdType.MESH
F32, BF16 = jnp.float32, jnp.bfloat16
INNER = 512
TILE = 128
LANES = 128


def tables():
    token = np.arange(INNER, dtype=np.float64)[:, None]
    freq = np.arange(INNER, dtype=np.float64)[None, :] + 0.5
    angle = 2.0 * np.pi * ((token * freq) % (2 * INNER)) / (2 * INNER)
    forward = np.concatenate([np.cos(angle), -np.sin(angle)], axis=1)
    inverse = forward.T / INNER

    def split(table):
        high = table.astype(ml_dtypes.bfloat16)
        low = (table - high.astype(np.float64)).astype(ml_dtypes.bfloat16)
        return np.concatenate([high, low], axis=0)

    return split(forward), split(inverse)


def kernel(
    n,
    nz,
    handoff,
    gate,
    source,
    filt,
    decay,
    forward_hbm,
    inverse_hbm,
    out_gate,
    out_source,
    out_filter,
    src_v,
    gate_v,
    filt_v,
    decay_v,
    forward_v,
    inverse_v,
    grad_v,
    mod_v,
    send_in,
    recv_in,
    spec,
    prod,
    send_out,
    recv_out,
    og_v,
    os_v,
    of_v,
    local_sem,
    pipe_send,
    pipe_recv,
    in_send,
    in_recv,
    out_send,
    out_recv,
):
    me = lax.axis_index("seq")
    mz = lax.axis_index("pipe")
    above, below = lax.rem(mz + 1, nz), lax.rem(mz + nz - 1, nz)
    width = src_v.shape[1]
    chans = width // n
    chunks = width // LANES
    per_chunk = LANES // chans
    group = INNER // TILE
    blocks = n // group
    rows = blocks * chans

    loads = [
        pltpu.make_async_copy(source.at[0], src_v, local_sem.at[0]),
        pltpu.make_async_copy(filt.at[0], filt_v, local_sem.at[1]),
        pltpu.make_async_copy(decay, decay_v, local_sem.at[2]),
        pltpu.make_async_copy(gate.at[0], gate_v, local_sem.at[3]),
        pltpu.make_async_copy(forward_hbm, forward_v, local_sem.at[4]),
        pltpu.make_async_copy(inverse_hbm, inverse_v, local_sem.at[5]),
    ]
    for load in loads:
        load.start()

    barrier = pltpu.get_barrier_semaphore()

    def greet(i, carry):
        pl.semaphore_signal(
            barrier, inc=1, device_id={"seq": lax.rem(me + i, n)}, device_id_type=MESH
        )
        return carry

    pl.semaphore_signal(barrier, inc=1, device_id={"pipe": above}, device_id_type=MESH)
    lax.fori_loop(1, n, greet, 0)

    def by_channel(value):
        return value.astype(F32).T.astype(BF16).reshape(-1, chans, TILE)

    loads[0].wait()
    send_in[0] = by_channel(src_v[...])
    recv_in[0, me] = send_in[0, me]

    pl.semaphore_wait(barrier, n)

    def pipe_copy(q):
        at = pl.multiple_of(lax.rem(q + me, chunks) * LANES, LANES)
        return pltpu.make_async_remote_copy(
            src_ref=handoff.at[0, :, pl.ds(at, LANES)],
            dst_ref=grad_v.at[:, pl.ds(at, LANES)],
            send_sem=pipe_send.at[q],
            recv_sem=pipe_recv.at[q],
            device_id={"pipe": below},
            device_id_type=MESH,
        )

    for q in range(chunks):
        pipe_copy(q).start()

    def exchange(src, dst, which, send_sems, recv_sems, dest):
        pltpu.make_async_remote_copy(
            src_ref=src.at[which, dest],
            dst_ref=dst.at[which, me],
            send_sem=send_sems.at[which],
            recv_sem=recv_sems.at[which],
            device_id={"seq": dest},
            device_id_type=MESH,
        ).start()

    def whole(src, dst, which, send_sems, recv_sems):
        return pltpu.make_async_remote_copy(
            src_ref=src.at[which, pl.ds(0, n - 1)],
            dst_ref=dst.at[which, pl.ds(0, n - 1)],
            send_sem=send_sems.at[which],
            recv_sem=recv_sems.at[which],
            device_id={"seq": lax.rem(me + 1, n)},
            device_id_type=MESH,
        )

    def send_all(which):
        def step(i, carry):
            exchange(send_in, recv_in, which, in_send, in_recv, lax.rem(me + i, n))
            return carry

        lax.fori_loop(1, n, step, 0)

    send_all(0)

    loads[1].wait()
    loads[2].wait()
    rates = decay_v[...]
    steps = (lax.broadcasted_iota(jnp.int32, (TILE, width), 0) + me * TILE).astype(F32)
    mod_v[...] = jnp.sqrt(2.0 * rates) * jnp.exp(-rates * steps)
    send_in[1] = by_channel(filt_v[...].astype(F32) * mod_v[...])
    recv_in[1, me] = send_in[1, me]
    send_all(1)

    loads[3].wait()
    for q in range(chunks):
        pipe_copy(q).wait_recv()
        chunk = lax.rem(q + me, chunks)
        cols = pl.ds(pl.multiple_of(chunk * LANES, LANES), LANES)
        product = grad_v[:, cols].astype(F32) * gate_v[:, cols].astype(F32)
        send_in[2, pl.ds(chunk * per_chunk, per_chunk)] = by_channel(product.astype(BF16))

        def step(i, carry):
            dest = chunk * per_chunk + lax.rem(me + i, per_chunk)

            @pl.when(dest != me)
            def _():
                exchange(send_in, recv_in, 2, in_send, in_recv, dest)

            return carry

        lax.fori_loop(0, per_chunk, step, 0)
    recv_in[2, me] = send_in[2, me]

    def forward(which):
        block = recv_in[which].reshape(blocks, group, chans, TILE)
        left = jnp.concatenate([block[:, j] for j in range(group)], axis=-1).reshape(rows, INNER)
        for at in range(0, 2 * INNER, 256):
            spec[which, :, at : at + 256] = jnp.dot(
                left, forward_v[0:INNER, at : at + 256], preferred_element_type=F32
            ) + jnp.dot(
                left, forward_v[INNER : 2 * INNER, at : at + 256], preferred_element_type=F32
            )

    def multiply(kept, other, correlate):
        def step(g, carry):
            at = pl.multiple_of(g * LANES, LANES)
            real, imag = pl.ds(at, LANES), pl.ds(pl.multiple_of(at + INNER, LANES), LANES)
            lane = lax.broadcasted_iota(jnp.int32, (8, LANES), 1)
            sign = (1 - 2 * lax.rem(lane, 2)).astype(F32)
            for half in range(0, chans, 8):
                part = [pl.ds(b * chans + half, 8) for b in range(blocks)]
                raw = [(spec[kept, part[b], real], spec[kept, part[b], imag]) for b in range(blocks)]
                fold = [raw[0]]
                for b in range(1, blocks):
                    before = raw[b - 1]
                    fold.append((raw[b][0] - sign * before[1], raw[b][1] + sign * before[0]))
                right = [
                    (spec[other, part[b], real], spec[other, part[b], imag]) for b in range(blocks)
                ]
                for i in range(blocks):
                    total_r = total_i = None
                    for j in range(i, blocks) if correlate else range(i + 1):
                        kr, ki = fold[j - i] if correlate else fold[i - j]
                        br, bi = right[j]
                        if correlate:
                            term_r, term_i = kr * br + ki * bi, kr * bi - ki * br
                        else:
                            term_r, term_i = kr * br - ki * bi, kr * bi + ki * br
                        total_r = term_r if total_r is None else total_r + term_r
                        total_i = term_i if total_i is None else total_i + term_i
                    prod[part[i], real] = total_r
                    prod[part[i], imag] = total_i
            return carry

        lax.fori_loop(0, INNER // LANES, step, 0)

    def inverse(which):
        left = prod[...].astype(BF16)
        half = 2 * INNER
        for at in range(0, INNER, 256):
            result = jnp.dot(
                left, inverse_v[0:half, at : at + 256], preferred_element_type=F32
            ) + jnp.dot(left, inverse_v[half : 2 * half, at : at + 256], preferred_element_type=F32)
            result = result.astype(BF16)
            for j in range(256 // TILE):
                piece = result[:, j * TILE : (j + 1) * TILE].reshape(blocks, chans, TILE)
                for b in range(blocks):
                    send_out[which, b * group + at // TILE + j] = piece[b]
        recv_out[which, me] = send_out[which, me]

        def step(i, carry):
            exchange(send_out, recv_out, which, out_send, out_recv, lax.rem(me + i, n))
            return carry

        lax.fori_loop(1, n, step, 0)

    loads[4].wait()
    loads[5].wait()
    whole(send_in, recv_in, 0, in_send, in_recv).wait_recv()
    forward(0)
    whole(send_in, recv_in, 1, in_send, in_recv).wait_recv()
    forward(1)
    multiply(1, 0, False)
    inverse(0)
    whole(send_in, recv_in, 2, in_send, in_recv).wait_recv()
    forward(2)
    multiply(1, 2, True)
    inverse(1)
    multiply(0, 2, True)
    inverse(2)

    def by_token(which):
        return recv_out[which].reshape(width, TILE).astype(F32).T

    whole(send_out, recv_out, 0, out_send, out_recv).wait_recv()
    og_v[...] = (grad_v[...].astype(F32) * by_token(0)).astype(BF16)
    stores = [pltpu.make_async_copy(og_v, out_gate.at[0], local_sem.at[6])]
    stores[0].start()
    whole(send_out, recv_out, 1, out_send, out_recv).wait_recv()
    os_v[...] = by_token(1).astype(BF16)
    stores.append(pltpu.make_async_copy(os_v, out_source.at[0], local_sem.at[7]))
    stores[1].start()
    whole(send_out, recv_out, 2, out_send, out_recv).wait_recv()
    of_v[...] = by_token(2) * mod_v[...]
    stores.append(pltpu.make_async_copy(of_v, out_filter.at[0], local_sem.at[8]))
    stores[2].start()

    for q in range(chunks):
        pipe_copy(q).wait_send()
    for which in range(3):
        whole(send_in, recv_in, which, in_send, in_recv).wait_send()
        whole(send_out, recv_out, which, out_send, out_recv).wait_send()
    for store in stores:
        store.wait()


def local(n, nz, handoff, gate_input, source, long_filter, decay_rates):
    forward_table, inverse_table = tables()
    _, tokens, width = source.shape
    chans = width // n
    rows = n * TILE // INNER * chans
    block = (tokens, width)
    return pl.pallas_call(
        functools.partial(kernel, n, nz),
        out_shape=(
            jax.ShapeDtypeStruct(source.shape, BF16),
            jax.ShapeDtypeStruct(source.shape, BF16),
            jax.ShapeDtypeStruct(source.shape, F32),
        ),
        in_specs=[pl.BlockSpec(memory_space=pl.ANY)] * 7,
        out_specs=[pl.BlockSpec(memory_space=pl.ANY)] * 3,
        scratch_shapes=[
            pltpu.VMEM(block, BF16),
            pltpu.VMEM(block, BF16),
            pltpu.VMEM(block, BF16),
            pltpu.VMEM((1, width), F32),
            pltpu.VMEM(forward_table.shape, BF16),
            pltpu.VMEM(inverse_table.shape, BF16),
            pltpu.VMEM(block, BF16),
            pltpu.VMEM(block, F32),
            pltpu.VMEM((3, n, chans, TILE), BF16),
            pltpu.VMEM((3, n, chans, TILE), BF16),
            pltpu.VMEM((3, rows, 2 * INNER), F32),
            pltpu.VMEM((rows, 2 * INNER), F32),
            pltpu.VMEM((3, n, chans, TILE), BF16),
            pltpu.VMEM((3, n, chans, TILE), BF16),
            pltpu.VMEM(block, BF16),
            pltpu.VMEM(block, BF16),
            pltpu.VMEM(block, F32),
            pltpu.SemaphoreType.DMA((9,)),
            pltpu.SemaphoreType.DMA((width // LANES,)),
            pltpu.SemaphoreType.DMA((width // LANES,)),
            pltpu.SemaphoreType.DMA((3,)),
            pltpu.SemaphoreType.DMA((3,)),
            pltpu.SemaphoreType.DMA((3,)),
            pltpu.SemaphoreType.DMA((3,)),
        ],
        compiler_params=pltpu.CompilerParams(
            collective_id=0, has_side_effects=True, vmem_limit_bytes=60 * 1024 * 1024
        ),
        cost_estimate=pl.CostEstimate(
            flops=2 * 6 * rows * 4 * INNER * INNER, bytes_accessed=6 << 20, transcendentals=0
        ),
    )(
        handoff,
        gate_input,
        source,
        long_filter,
        decay_rates,
        jnp.asarray(forward_table),
        jnp.asarray(inverse_table),
    )


def solution(mesh):
    tokens = P("pipe", "seq", None)
    return jax.shard_map(
        functools.partial(local, mesh.shape["seq"], mesh.shape["pipe"]),
        mesh=mesh,
        in_specs=(tokens, tokens, tokens, tokens, P("pipe", None)),
        out_specs=(tokens, tokens, tokens),
        check_vma=False,
    )
```

profile of v0, /device:TPU:1, one launch (start us, length us, event | category | flops | bytes accessed | tf_op | source)
XLA Modules:
  0.0 35.6 jit_solution(359759701283203293)
XLA Ops:
  0.6 30.1 %shard_map.94 = (bf16[1,128,512]{2,1,0:T(8,128)(2,1)}, bf16[1,128,512]{2,1,0:T(8,128)(2,1)}, f32[1,128,512]{2,1,0:T(8,128)}) custom-call(bf16[1,128,512]{2,1,0:T(8,128)(2,1)} %handoff.1, bf16[1,128,512]{2,1,0:T(8,128)(2,1)} %gate.1, bf16[1,128,512]{2,1,0:T(8,128)(2,1)} %source.1, bf16[1,128,512]{2,1,0:T(8,128)(2,1)} %filt.1, f32[1,512]{1,0:T(1,128)} %decay.1, ...), custom_call_target="tpu_custom_call" | custom-call | flops 1610612736 | bytes 6291456 | tf_op jit(solution)/shard_map/pallas_call | solution.py:295
  30.8 1.6 %copy.13 = bf16[1,128,512]{2,1,0:T(8,128)(2,1)} copy(bf16[1,128,512]{2,1,0:T(8,128)(2,1)} %get-tuple-element.6) | data formatting | bytes 262144
  32.3 1.6 %copy.14 = bf16[1,128,512]{2,1,0:T(8,128)(2,1)} copy(bf16[1,128,512]{2,1,0:T(8,128)(2,1)} %get-tuple-element.7) | data formatting | bytes 262144
  33.9 1.7 %copy.15 = f32[1,128,512]{2,1,0:T(8,128)} copy(f32[1,128,512]{2,1,0:T(8,128)} %get-tuple-element.8) | data formatting | bytes 524288
where the time goes:
time: 35.8 us; the launch traced here: 35.6 us
  Pallas kernels  30.1 us (84%)
  local copies, waits for them, and re-layouts  4.81 us (13%)
  between operations  0.64 us (2%)
    pallas_call x1, Pallas kernels, local(): pl.pallas_call(functools.partial(kernel, n, nz), out_shape=(jax.ShapeDtyp...  30.1 us
    unnamed x3, local copies, waits for them, and re-layouts  4.81 us

commit v1 on v0

--- a/solution.py
+++ b/solution.py
@@ -41,9 +41,9 @@
     decay,
     forward_hbm,
     inverse_hbm,
-    out_gate,
-    out_source,
-    out_filter,
+    og_v,
+    os_v,
+    of_v,
     src_v,
     gate_v,
     filt_v,
@@ -58,10 +58,8 @@
     prod,
     send_out,
     recv_out,
-    og_v,
-    os_v,
-    of_v,
     local_sem,
+    pipe_ready,
     pipe_send,
     pipe_recv,
     in_send,
@@ -99,7 +97,16 @@
         )
         return carry
 
-    pl.semaphore_signal(barrier, inc=1, device_id={"pipe": above}, device_id_type=MESH)
+    first, last = mz == 0, mz == nz - 1
+
+    @pl.when(jnp.logical_not(last))
+    def _():
+        pl.semaphore_signal(barrier, inc=1, device_id={"pipe": above}, device_id_type=MESH)
+
+    @pl.when(first)
+    def _():
+        pl.semaphore_signal(barrier, inc=1, device_id={"pipe": below}, device_id_type=MESH)
+
     lax.fori_loop(1, n, greet, 0)
 
     def by_channel(value):
@@ -109,7 +116,7 @@
     send_in[0] = by_channel(src_v[...])
     recv_in[0, me] = send_in[0, me]
 
-    pl.semaphore_wait(barrier, n)
+    pl.semaphore_wait(barrier, n - 1 + jnp.where(first, 0, 1) + jnp.where(last, 1, 0))
 
     def pipe_copy(q):
         at = pl.multiple_of(lax.rem(q + me, chunks) * LANES, LANES)
@@ -122,8 +129,15 @@
             device_id_type=MESH,
         )
 
-    for q in range(chunks):
-        pipe_copy(q).start()
+    def pass_on():
+        for q in range(chunks):
+            pipe_copy(q).start()
+
+    pl.when(jnp.logical_not(first))(pass_on)
+
+    @pl.when(last)
+    def _():
+        pl.semaphore_signal(pipe_ready, inc=1, device_id={"pipe": above}, device_id_type=MESH)
 
     def exchange(src, dst, which, send_sems, recv_sems, dest):
         pltpu.make_async_remote_copy(
@@ -182,6 +196,12 @@
 
         lax.fori_loop(0, per_chunk, step, 0)
     recv_in[2, me] = send_in[2, me]
+
+    @pl.when(first)
+    def _():
+        pl.semaphore_wait(pipe_ready, 1)
+        pass_on()
+
 
     def forward(which):
         block = recv_in[which].reshape(blocks, group, chans, TILE)
@@ -266,22 +286,26 @@
 
     whole(send_out, recv_out, 0, out_send, out_recv).wait_recv()
     og_v[...] = (grad_v[...].astype(F32) * by_token(0)).astype(BF16)
-    stores = [pltpu.make_async_copy(og_v, out_gate.at[0], local_sem.at[6])]
-    stores[0].start()
     whole(send_out, recv_out, 1, out_send, out_recv).wait_recv()
     os_v[...] = by_token(1).astype(BF16)
-    stores.append(pltpu.make_async_copy(os_v, out_source.at[0], local_sem.at[7]))
-    stores[1].start()
     whole(send_out, recv_out, 2, out_send, out_recv).wait_recv()
     of_v[...] = by_token(2) * mod_v[...]
-    stores.append(pltpu.make_async_copy(of_v, out_filter.at[0], local_sem.at[8]))
-    stores[2].start()
 
     for q in range(chunks):
         pipe_copy(q).wait_send()
     for which in range(3):
         whole(send_in, recv_in, which, in_send, in_recv).wait_send()
         whole(send_out, recv_out, which, out_send, out_recv).wait_send()
+
+
+def write_out(gate_v, source_v, filter_v, out_gate, out_source, out_filter, sems):
+    stores = [
+        pltpu.make_async_copy(filter_v, out_filter.at[0], sems.at[0]),
+        pltpu.make_async_copy(source_v, out_source.at[0], sems.at[1]),
+        pltpu.make_async_copy(gate_v, out_gate.at[0], sems.at[2]),
+    ]
+    for store in stores:
+        store.start()
     for store in stores:
         store.wait()
 
@@ -292,15 +316,16 @@
     chans = width // n
     rows = n * TILE // INNER * chans
     block = (tokens, width)
-    return pl.pallas_call(
+    hbm = lambda value: pltpu.with_memory_space_constraint(value, pltpu.HBM)
+    results = pl.pallas_call(
         functools.partial(kernel, n, nz),
         out_shape=(
-            jax.ShapeDtypeStruct(source.shape, BF16),
-            jax.ShapeDtypeStruct(source.shape, BF16),
-            jax.ShapeDtypeStruct(source.shape, F32),
+            pltpu.VMEM(block, BF16),
+            pltpu.VMEM(block, BF16),
+            pltpu.VMEM(block, F32),
         ),
-        in_specs=[pl.BlockSpec(memory_space=pl.ANY)] * 7,
-        out_specs=[pl.BlockSpec(memory_space=pl.ANY)] * 3,
+        in_specs=[pl.BlockSpec(memory_space=pltpu.HBM)] * 7,
+        out_specs=[pl.BlockSpec(memory_space=pltpu.VMEM)] * 3,
         scratch_shapes=[
             pltpu.VMEM(block, BF16),
             pltpu.VMEM(block, BF16),
@@ -316,10 +341,8 @@
             pltpu.VMEM((rows, 2 * INNER), F32),
             pltpu.VMEM((3, n, chans, TILE), BF16),
             pltpu.VMEM((3, n, chans, TILE), BF16),
-            pltpu.VMEM(block, BF16),
-            pltpu.VMEM(block, BF16),
-            pltpu.VMEM(block, F32),
-            pltpu.SemaphoreType.DMA((9,)),
+            pltpu.SemaphoreType.DMA((6,)),
+            pltpu.SemaphoreType.REGULAR,
             pltpu.SemaphoreType.DMA((width // LANES,)),
             pltpu.SemaphoreType.DMA((width // LANES,)),
             pltpu.SemaphoreType.DMA((3,)),
@@ -328,20 +351,28 @@
             pltpu.SemaphoreType.DMA((3,)),
         ],
         compiler_params=pltpu.CompilerParams(
-            collective_id=0, has_side_effects=True, vmem_limit_bytes=60 * 1024 * 1024
+            collective_id=0, has_side_effects=True, vmem_limit_bytes=40 * 1024 * 1024
         ),
         cost_estimate=pl.CostEstimate(
             flops=2 * 6 * rows * 4 * INNER * INNER, bytes_accessed=6 << 20, transcendentals=0
         ),
     )(
-        handoff,
-        gate_input,
-        source,
-        long_filter,
-        decay_rates,
-        jnp.asarray(forward_table),
-        jnp.asarray(inverse_table),
+        hbm(handoff),
+        hbm(gate_input),
+        hbm(source),
+        hbm(long_filter),
+        hbm(decay_rates),
+        hbm(jnp.asarray(forward_table)),
+        hbm(jnp.asarray(inverse_table)),
     )
+    return pl.pallas_call(
+        write_out,
+        out_shape=tuple(jax.ShapeDtypeStruct(source.shape, r.dtype) for r in results),
+        in_specs=[pl.BlockSpec(memory_space=pltpu.VMEM)] * 3,
+        out_specs=[pl.BlockSpec(memory_space=pltpu.HBM)] * 3,
+        scratch_shapes=[pltpu.SemaphoreType.DMA((3,))],
+        compiler_params=pltpu.CompilerParams(vmem_limit_bytes=4 * 1024 * 1024),
+    )(*[pltpu.with_memory_space_constraint(r, pltpu.VMEM) for r in results])
 
 
 def solution(mesh):

time: 35.8 us -> 28.2 us (0.79)
  local copies, waits for them, and re-layouts: 4.81 us -> 0 us
  Pallas kernels: 30.1 us -> 27.1 us
    unnamed x3 -> x0, local copies, waits for them, and re-layouts: 4.81 us -> none
    pallas_call x1 -> x2, Pallas kernels: 30.1 us -> 27.1 us  [the longest x1 26.3 us: local(): pl.pallas_call(functools.partial(kernel, n, nz), out_shape=(pltpu.VMEM(bl...]
where the time goes in v1:
time: 28.2 us; the launch traced here: 27.8 us
  Pallas kernels  27.1 us (96%)
  between operations  0.64 us (2%)
    pallas_call x1, Pallas kernels, local(): pl.pallas_call(functools.partial(kernel, n, nz), out_shape=(pltpu.VMEM(bl...  26.3 us
    pallas_call x1, Pallas kernels, local(): pl.pallas_call(write_out, out_shape=tuple((jax.ShapeDtypeStruct(source.sh...  0.81 us

profile of v1, /device:TPU:1, one launch (start us, length us, event | category | flops | bytes accessed | tf_op | source)
XLA Modules:
  0.0 27.8 jit_solution(1176380167819788040)
XLA Ops:
  0.6 26.3 %shard_map.94 = (bf16[128,512]{1,0:T(8,128)(2,1)S(1)}, bf16[128,512]{1,0:T(8,128)(2,1)S(1)}, f32[128,512]{1,0:T(8,128)S(1)}) custom-call(bf16[1,128,512]{2,1,0:T(8,128)(2,1)} %handoff.1, bf16[1,128,512]{2,1,0:T(8,128)(2,1)} %gate.1, bf16[1,128,512]{2,1,0:T(8,128)(2,1)} %source.1, bf16[1,128,512]{2,1,0:T(8,128)(2,1)} %filt.1, f32[1,512]{1,0:T(1,128)} %decay.1, ...), custom_call_target="tpu_custom_call" | custom-call | flops 1610612736 | bytes 6291456 | tf_op jit(solution)/shard_map/pallas_call | solution.py:320
  27.0 0.8 %shard_map.95 = (bf16[1,128,512]{2,1,0:T(8,128)(2,1)}, bf16[1,128,512]{2,1,0:T(8,128)(2,1)}, f32[1,128,512]{2,1,0:T(8,128)}) custom-call(bf16[128,512]{1,0:T(8,128)(2,1)S(1)} %get-tuple-element.6.gate_v, bf16[128,512]{1,0:T(8,128)(2,1)S(1)} %get-tuple-element.7.source_v, f32[128,512]{1,0:T(8,128)S(1)} %get-tuple-element.8.filter_v), custom_call_target="tpu_custom_call" | custom-call | tf_op jit(solution)/shard_map/pallas_call | solution.py:368

commit v2 on v1

--- a/solution.py
+++ b/solution.py
@@ -78,6 +78,39 @@
     blocks = n // group
     rows = blocks * chans
 
+    nx, ny, nc = n // 8, 4, 2
+    xs = [lax.rem(me // 8 + d, nx) for d in range(nx)]
+    ys = [lax.rem(lax.rem(me // nc, ny) + d, ny) for d in range(ny)]
+    cs = [lax.rem(lax.rem(me, nc) + d, nc) for d in range(nc)]
+
+    def hops(offset):
+        dx, dy, dc = offset
+        return min(dx, nx - dx) + min(dy, ny - dy) + 0.1 * dc
+
+    def index(offset):
+        dx, dy, dc = offset
+        return xs[dx] * (ny * nc) + ys[dy] * nc + cs[dc]
+
+    offsets = [(dx, dy, dc) for dx in range(nx) for dy in range(ny) for dc in range(nc)]
+    offsets = sorted(offsets, key=hops, reverse=True)[:-1]
+    turns = sorted(range(nx), key=lambda d: min(d, nx - d), reverse=True)
+
+    barrier = pltpu.get_barrier_semaphore()
+
+    for offset in offsets:
+        pl.semaphore_signal(barrier, inc=1, device_id={"seq": index(offset)}, device_id_type=MESH)
+
+    first, last = mz == 0, mz == nz - 1
+
+    @pl.when(jnp.logical_not(last))
+    def _():
+        pl.semaphore_signal(barrier, inc=1, device_id={"pipe": above}, device_id_type=MESH)
+
+    @pl.when(first)
+    def _():
+        pl.semaphore_signal(barrier, inc=1, device_id={"pipe": below}, device_id_type=MESH)
+
+
     loads = [
         pltpu.make_async_copy(source.at[0], src_v, local_sem.at[0]),
         pltpu.make_async_copy(filt.at[0], filt_v, local_sem.at[1]),
@@ -89,26 +122,6 @@
     for load in loads:
         load.start()
 
-    barrier = pltpu.get_barrier_semaphore()
-
-    def greet(i, carry):
-        pl.semaphore_signal(
-            barrier, inc=1, device_id={"seq": lax.rem(me + i, n)}, device_id_type=MESH
-        )
-        return carry
-
-    first, last = mz == 0, mz == nz - 1
-
-    @pl.when(jnp.logical_not(last))
-    def _():
-        pl.semaphore_signal(barrier, inc=1, device_id={"pipe": above}, device_id_type=MESH)
-
-    @pl.when(first)
-    def _():
-        pl.semaphore_signal(barrier, inc=1, device_id={"pipe": below}, device_id_type=MESH)
-
-    lax.fori_loop(1, n, greet, 0)
-
     def by_channel(value):
         return value.astype(F32).T.astype(BF16).reshape(-1, chans, TILE)
 
@@ -119,7 +132,7 @@
     pl.semaphore_wait(barrier, n - 1 + jnp.where(first, 0, 1) + jnp.where(last, 1, 0))
 
     def pipe_copy(q):
-        at = pl.multiple_of(lax.rem(q + me, chunks) * LANES, LANES)
+        at = pl.multiple_of(xs[turns[q]] * LANES, LANES)
         return pltpu.make_async_remote_copy(
             src_ref=handoff.at[0, :, pl.ds(at, LANES)],
             dst_ref=grad_v.at[:, pl.ds(at, LANES)],
@@ -160,11 +173,8 @@
         )
 
     def send_all(which):
-        def step(i, carry):
-            exchange(send_in, recv_in, which, in_send, in_recv, lax.rem(me + i, n))
-            return carry
-
-        lax.fori_loop(1, n, step, 0)
+        for offset in offsets:
+            exchange(send_in, recv_in, which, in_send, in_recv, index(offset))
 
     send_all(0)
 
@@ -180,21 +190,14 @@
     loads[3].wait()
     for q in range(chunks):
         pipe_copy(q).wait_recv()
-        chunk = lax.rem(q + me, chunks)
+        chunk = xs[turns[q]]
         cols = pl.ds(pl.multiple_of(chunk * LANES, LANES), LANES)
         product = grad_v[:, cols].astype(F32) * gate_v[:, cols].astype(F32)
         send_in[2, pl.ds(chunk * per_chunk, per_chunk)] = by_channel(product.astype(BF16))
 
-        def step(i, carry):
-            dest = chunk * per_chunk + lax.rem(me + i, per_chunk)
-
-            @pl.when(dest != me)
-            def _():
-                exchange(send_in, recv_in, 2, in_send, in_recv, dest)
-
-            return carry
-
-        lax.fori_loop(0, per_chunk, step, 0)
+        for offset in offsets:
+            if offset[0] == turns[q]:
+                exchange(send_in, recv_in, 2, in_send, in_recv, index(offset))
     recv_in[2, me] = send_in[2, me]
 
     @pl.when(first)
@@ -260,11 +263,8 @@
                     send_out[which, b * group + at // TILE + j] = piece[b]
         recv_out[which, me] = send_out[which, me]
 
-        def step(i, carry):
-            exchange(send_out, recv_out, which, out_send, out_recv, lax.rem(me + i, n))
-            return carry
-
-        lax.fori_loop(1, n, step, 0)
+        for offset in offsets:
+            exchange(send_out, recv_out, which, out_send, out_recv, index(offset))
 
     loads[4].wait()
     loads[5].wait()

time: 28.2 us -> 27 us (0.957); the launches traced: 27.8 us -> 26.9 us
  Pallas kernels: 27.1 us -> 26.3 us
    pallas_call x1, Pallas kernels: 26.3 us -> 25.4 us  [local(): pl.pallas_call(functools.partial(kernel, n, nz), out_shape=(pltpu.VMEM(bl...]
where the time goes in v2:
time: 27 us; the launch traced here: 26.9 us
  Pallas kernels  26.3 us (97%)
  between operations  0.64 us (2%)
    pallas_call x1, Pallas kernels, local(): pl.pallas_call(functools.partial(kernel, n, nz), out_shape=(pltpu.VMEM(bl...  25.4 us
    pallas_call x1, Pallas kernels, local(): pl.pallas_call(write_out, out_shape=tuple((jax.ShapeDtypeStruct(source.sh...  0.81 us

profile of v2, /device:TPU:1, one launch (start us, length us, event | category | flops | bytes accessed | tf_op | source)
XLA Modules:
  0.0 26.9 jit_solution(14898788447750695218)
XLA Ops:
  0.6 25.4 %shard_map.94 = (bf16[128,512]{1,0:T(8,128)(2,1)S(1)}, bf16[128,512]{1,0:T(8,128)(2,1)S(1)}, f32[128,512]{1,0:T(8,128)S(1)}) custom-call(bf16[1,128,512]{2,1,0:T(8,128)(2,1)} %handoff.1, bf16[1,128,512]{2,1,0:T(8,128)(2,1)} %gate.1, bf16[1,128,512]{2,1,0:T(8,128)(2,1)} %source.1, bf16[1,128,512]{2,1,0:T(8,128)(2,1)} %filt.1, f32[1,512]{1,0:T(1,128)} %decay.1, ...), custom_call_target="tpu_custom_call" | custom-call | flops 1610612736 | bytes 6291456 | tf_op jit(solution)/shard_map/pallas_call | solution.py:320
  26.1 0.8 %shard_map.95 = (bf16[1,128,512]{2,1,0:T(8,128)(2,1)}, bf16[1,128,512]{2,1,0:T(8,128)(2,1)}, f32[1,128,512]{2,1,0:T(8,128)}) custom-call(bf16[128,512]{1,0:T(8,128)(2,1)S(1)} %get-tuple-element.6.gate_v, bf16[128,512]{1,0:T(8,128)(2,1)S(1)} %get-tuple-element.7.source_v, f32[128,512]{1,0:T(8,128)S(1)} %get-tuple-element.8.filter_v), custom_call_target="tpu_custom_call" | custom-call | tf_op jit(solution)/shard_map/pallas_call | solution.py:368

commit v3 on v2

v3 whole, which is shorter than its diff:
```python
import functools

import jax
import jax.numpy as jnp
import ml_dtypes
import numpy as np
from jax import lax
from jax.experimental import pallas as pl
from jax.experimental.pallas import tpu as pltpu
from jax.sharding import PartitionSpec as P

MESH = pl.DeviceIdType.MESH
F32, BF16 = jnp.float32, jnp.bfloat16
INNER = 512
TILE = 128
LANES = 128
SOURCE, KERNEL, GRAD = 0, 1, 2


def tables():
    token = np.arange(INNER, dtype=np.float64)[:, None]
    freq = np.arange(INNER, dtype=np.float64)[None, :] + 0.5
    angle = 2.0 * np.pi * ((token * freq) % (2 * INNER)) / (2 * INNER)
    forward = np.concatenate([np.cos(angle), -np.sin(angle)], axis=1)
    inverse = forward.T / INNER

    def split(table):
        high = table.astype(ml_dtypes.bfloat16)
        low = (table - high.astype(np.float64)).astype(ml_dtypes.bfloat16)
        return np.concatenate([high, low], axis=0)

    return split(forward), split(inverse)


def kernel(
    n,
    nz,
    handoff,
    gate,
    source,
    filt,
    decay,
    forward_hbm,
    inverse_hbm,
    og_v,
    pair_v,
    mod_v,
    src_v,
    gate_v,
    filt_v,
    decay_v,
    forward_v,
    inverse_v,
    grad_v,
    send_first,
    recv_first,
    send_grad,
    recv_grad,
    spec,
    prod,
    send_conv,
    recv_conv,
    send_pair,
    local_sem,
    pipe_ready,
    all_in,
    pipe_send,
    pipe_recv,
    send_sem,
    recv_sem,
):
    me = lax.axis_index("seq")
    mz = lax.axis_index("pipe")
    above, below = lax.rem(mz + 1, nz), lax.rem(mz + nz - 1, nz)
    width = src_v.shape[1]
    chans = width // n
    chunks = width // LANES
    per_chunk = LANES // chans
    group = INNER // TILE
    blocks = n // group
    rows = blocks * chans

    nx, ny, nc = n // 8, 4, 2
    xs = [lax.rem(me // 8 + d, nx) for d in range(nx)]
    ys = [lax.rem(lax.rem(me // nc, ny) + d, ny) for d in range(ny)]
    cs = [lax.rem(lax.rem(me, nc) + d, nc) for d in range(nc)]

    def hops(offset):
        dx, dy, dc = offset
        return min(dx, nx - dx) + min(dy, ny - dy) + 0.1 * dc

    def index(offset):
        dx, dy, dc = offset
        return xs[dx] * (ny * nc) + ys[dy] * nc + cs[dc]

    offsets = [(dx, dy, dc) for dx in range(nx) for dy in range(ny) for dc in range(nc)]
    offsets = sorted(offsets, key=hops, reverse=True)[:-1]
    turns = sorted(range(nx), key=lambda d: min(d, nx - d), reverse=True)

    core = lax.rem(me, nc)
    second = me - core + 1
    sibling = me + 1 - 2 * core
    first, last = mz == 0, mz == nz - 1
    barrier = pltpu.get_barrier_semaphore()

    @pl.when(jnp.logical_not(last))
    def _():
        pl.semaphore_signal(
            barrier, inc=1, device_id={"pipe": above, "seq": second}, device_id_type=MESH
        )

    pl.semaphore_signal(barrier, inc=1, device_id={"seq": sibling}, device_id_type=MESH)
    for dx, dy, dc in offsets:
        if dc == 0:
            at = xs[dx] * (ny * nc) + ys[dy] * nc
            pl.semaphore_signal(barrier, inc=1, device_id={"seq": at}, device_id_type=MESH)

    @pl.when(first)
    def _():
        pl.semaphore_signal(
            barrier, inc=1, device_id={"pipe": below, "seq": second}, device_id_type=MESH
        )

    loads = [
        pltpu.make_async_copy(source.at[0], src_v, local_sem.at[0]),
        pltpu.make_async_copy(filt.at[0], filt_v, local_sem.at[1]),
        pltpu.make_async_copy(decay, decay_v, local_sem.at[2]),
        pltpu.make_async_copy(gate.at[0], gate_v, local_sem.at[3]),
        pltpu.make_async_copy(forward_hbm, forward_v, local_sem.at[4]),
        pltpu.make_async_copy(inverse_hbm, inverse_v, local_sem.at[5]),
    ]
    for load in loads:
        load.start()

    def pipe_copy(q):
        at = pl.multiple_of(xs[turns[q]] * LANES, LANES)
        return pltpu.make_async_remote_copy(
            src_ref=handoff.at[0, :, pl.ds(at, LANES)],
            dst_ref=grad_v.at[:, pl.ds(at, LANES)],
            send_sem=pipe_send.at[q],
            recv_sem=pipe_recv.at[q],
            device_id={"pipe": below},
            device_id_type=MESH,
        )

    def pass_on():
        for q in range(chunks):
            pipe_copy(q).start()

    @pl.when(core == 1)
    def _():
        pl.semaphore_wait(barrier, 1 + jnp.where(first, 0, 2) + jnp.where(last, 2, 0))

        @pl.when(jnp.logical_not(first))
        def _():
            pl.semaphore_signal(pipe_ready, inc=1, device_id={"seq": sibling}, device_id_type=MESH)
            pass_on()

        @pl.when(last)
        def _():
            for to in (second - 1, second):
                pl.semaphore_signal(
                    pipe_ready, inc=1, device_id={"pipe": above, "seq": to}, device_id_type=MESH
                )

    @pl.when(jnp.logical_and(core == 0, jnp.logical_not(first)))
    def _():
        pl.semaphore_wait(pipe_ready, 1)
        pass_on()

    def by_channel(value):
        return value.astype(F32).T.astype(BF16).reshape(-1, chans, TILE)

    loads[0].wait()
    send_first[:, 0] = by_channel(src_v[...])
    loads[1].wait()
    loads[2].wait()
    rates = decay_v[...]
    steps = (lax.broadcasted_iota(jnp.int32, (TILE, width), 0) + me * TILE).astype(F32)
    mod_v[...] = jnp.sqrt(2.0 * rates) * jnp.exp(-rates * steps)
    send_first[:, 1] = by_channel(filt_v[...].astype(F32) * mod_v[...])
    recv_first[me] = send_first[me]

    @pl.when(core == 0)
    def _():
        pl.semaphore_wait(barrier, n - 1)
        pl.semaphore_signal(all_in, inc=1, device_id={"seq": sibling}, device_id_type=MESH)

    @pl.when(core == 1)
    def _():
        pl.semaphore_wait(all_in, 1)

    def exchange(src, dst, sem, places):
        for offset in places:
            dest = index(offset)
            pltpu.make_async_remote_copy(
                src_ref=src.at[dest],
                dst_ref=dst.at[me],
                send_sem=send_sem.at[sem],
                recv_sem=recv_sem.at[sem],
                device_id={"seq": dest},
                device_id_type=MESH,
            ).start()

    def whole(src, dst, sem):
        return pltpu.make_async_remote_copy(
            src_ref=src.at[pl.ds(0, n - 1)],
            dst_ref=dst.at[pl.ds(0, n - 1)],
            send_sem=send_sem.at[sem],
            recv_sem=recv_sem.at[sem],
            device_id={"seq": index((0, 0, 1))},
            device_id_type=MESH,
        )

    exchange(send_first, recv_first, 0, offsets)

    loads[3].wait()
    for q in range(chunks):
        pipe_copy(q).wait_recv()
        chunk = xs[turns[q]]
        cols = pl.ds(pl.multiple_of(chunk * LANES, LANES), LANES)
        product = grad_v[:, cols].astype(F32) * gate_v[:, cols].astype(F32)
        send_grad[pl.ds(chunk * per_chunk, per_chunk)] = by_channel(product.astype(BF16))
        exchange(send_grad, recv_grad, 1, [o for o in offsets if o[0] == turns[q]])
    recv_grad[me] = send_grad[me]

    @pl.when(first)
    def _():
        pl.semaphore_wait(pipe_ready, 1)
        pass_on()

    def lines(block):
        return jnp.concatenate([block[:, j] for j in range(group)], axis=-1).reshape(rows, INNER)

    def forward(left, place):
        count = left.shape[0] // rows
        for at in (0, 512, 256, 768):
            result = jnp.dot(
                left, forward_v[0:INNER, at : at + 256], preferred_element_type=F32
            ) + jnp.dot(
                left, forward_v[INNER : 2 * INNER, at : at + 256], preferred_element_type=F32
            )
            for i in range(count):
                spec[place + i, :, at : at + 256] = result[i * rows : (i + 1) * rows]

    def multiply(kept, other, correlate, base):
        def step(g, carry):
            at = pl.multiple_of(g * LANES, LANES)
            real, imag = pl.ds(at, LANES), pl.ds(pl.multiple_of(at + INNER, LANES), LANES)
            lane = lax.broadcasted_iota(jnp.int32, (8, LANES), 1)
            sign = (1 - 2 * lax.rem(lane, 2)).astype(F32)
            for half in range(0, chans, 8):
                part = [pl.ds(b * chans + half, 8) for b in range(blocks)]
                raw = [(spec[kept, part[b], real], spec[kept, part[b], imag]) for b in range(blocks)]
                fold = [raw[0]]
                for b in range(1, blocks):
                    before = raw[b - 1]
                    fold.append((raw[b][0] - sign * before[1], raw[b][1] + sign * before[0]))
                right = [
                    (spec[other, part[b], real], spec[other, part[b], imag]) for b in range(blocks)
                ]
                for i in range(blocks):
                    total_r = total_i = None
                    for j in range(i, blocks) if correlate else range(i + 1):
                        kr, ki = fold[j - i] if correlate else fold[i - j]
                        br, bi = right[j]
                        if correlate:
                            term_r, term_i = kr * br + ki * bi, kr * bi - ki * br
                        else:
                            term_r, term_i = kr * br - ki * bi, kr * bi + ki * br
                        total_r = term_r if total_r is None else total_r + term_r
                        total_i = term_i if total_i is None else total_i + term_i
                    to = pl.ds(base + i * chans + half, 8)
                    prod[to, real] = total_r
                    prod[to, imag] = total_i
            return carry

        lax.fori_loop(0, INNER // LANES, step, 0, unroll=True)

    def inverse(count, store):
        left = prod[0 : count * rows].astype(BF16)
        half = 2 * INNER
        for at in range(0, INNER, 256):
            result = jnp.dot(
                left, inverse_v[0:half, at : at + 256], preferred_element_type=F32
            ) + jnp.dot(left, inverse_v[half : 2 * half, at : at + 256], preferred_element_type=F32)
            result = result.astype(BF16)
            for i in range(count):
                for j in range(256 // TILE):
                    piece = result[i * rows : (i + 1) * rows, j * TILE : (j + 1) * TILE]
                    piece = piece.reshape(blocks, chans, TILE)
                    for b in range(blocks):
                        store(i, b * group + at // TILE + j, piece[b])

    loads[4].wait()
    loads[5].wait()
    whole(send_first, recv_first, 0).wait_recv()
    block = recv_first[...].reshape(blocks, group, 2, chans, TILE)
    both = jnp.concatenate([lines(block[:, :, SOURCE]), lines(block[:, :, KERNEL])], axis=0)
    forward(both, SOURCE)
    multiply(KERNEL, SOURCE, False, 0)

    def store_conv(i, dest, piece):
        send_conv[dest] = piece

    inverse(1, store_conv)
    recv_conv[me] = send_conv[me]
    exchange(send_conv, recv_conv, 2, offsets)

    whole(send_grad, recv_grad, 1).wait_recv()
    forward(lines(recv_grad[...].reshape(blocks, group, chans, TILE)), GRAD)
    multiply(KERNEL, GRAD, True, 0)
    multiply(SOURCE, GRAD, True, rows)

    def store_pair(i, dest, piece):
        send_pair[dest, i] = piece

    inverse(2, store_pair)
    pair_v[me] = send_pair[me]
    exchange(send_pair, pair_v, 3, offsets)

    whole(send_conv, recv_conv, 2).wait_recv()
    turned = recv_conv[...].reshape(width, TILE).astype(F32).T
    og_v[...] = (grad_v[...].astype(F32) * turned).astype(BF16)

    for q in range(chunks):
        pipe_copy(q).wait_send()
    whole(send_first, recv_first, 0).wait_send()
    whole(send_grad, recv_grad, 1).wait_send()
    whole(send_conv, recv_conv, 2).wait_send()
    whole(send_pair, pair_v, 3).wait_send()
    whole(send_pair, pair_v, 3).wait_recv()


def finish(gate_v, pair_v, mod_v, out_gate, out_source, out_filter, source_v, filter_v, sems):
    width = mod_v.shape[1]
    chans = pair_v.shape[2]
    per_chunk = LANES // chans
    stores = []

    def store(src, dst):
        stores.append(pltpu.make_async_copy(src, dst, sems.at[len(stores)]))
        stores[-1].start()

    store(gate_v, out_gate.at[0])
    for q in range(width // LANES):
        cols = slice(q * LANES, (q + 1) * LANES)
        here = pair_v[q * per_chunk : (q + 1) * per_chunk]
        filter_v[:, cols] = here[:, 1].reshape(LANES, TILE).astype(F32).T * mod_v[:, cols]
        store(filter_v.at[:, cols], out_filter.at[0, :, cols])
        source_v[:, cols] = here[:, 0].reshape(LANES, TILE).astype(F32).T.astype(BF16)
        store(source_v.at[:, cols], out_source.at[0, :, cols])
    for started in stores:
        started.wait()


def local(n, nz, handoff, gate_input, source, long_filter, decay_rates):
    forward_table, inverse_table = tables()
    _, tokens, width = source.shape
    chans = width // n
    rows = n * TILE // INNER * chans
    block = (tokens, width)
    one, two = (n, chans, TILE), (n, 2, chans, TILE)
    hbm = lambda value: pltpu.with_memory_space_constraint(value, pltpu.HBM)
    results = pl.pallas_call(
        functools.partial(kernel, n, nz),
        out_shape=(pltpu.VMEM(block, BF16), pltpu.VMEM(two, BF16), pltpu.VMEM(block, F32)),
        in_specs=[pl.BlockSpec(memory_space=pltpu.HBM)] * 7,
        out_specs=[pl.BlockSpec(memory_space=pltpu.VMEM)] * 3,
        scratch_shapes=[
            pltpu.VMEM(block, BF16),
            pltpu.VMEM(block, BF16),
            pltpu.VMEM(block, BF16),
            pltpu.VMEM((1, width), F32),
            pltpu.VMEM(forward_table.shape, BF16),
            pltpu.VMEM(inverse_table.shape, BF16),
            pltpu.VMEM(block, BF16),
            pltpu.VMEM(two, BF16),
            pltpu.VMEM(two, BF16),
            pltpu.VMEM(one, BF16),
            pltpu.VMEM(one, BF16),
            pltpu.VMEM((3, rows, 2 * INNER), F32),
            pltpu.VMEM((2 * rows, 2 * INNER), F32),
            pltpu.VMEM(one, BF16),
            pltpu.VMEM(one, BF16),
            pltpu.VMEM(two, BF16),
            pltpu.SemaphoreType.DMA((6,)),
            pltpu.SemaphoreType.REGULAR,
            pltpu.SemaphoreType.REGULAR,
            pltpu.SemaphoreType.DMA((width // LANES,)),
            pltpu.SemaphoreType.DMA((width // LANES,)),
            pltpu.SemaphoreType.DMA((4,)),
            pltpu.SemaphoreType.DMA((4,)),
        ],
        compiler_params=pltpu.CompilerParams(
            collective_id=0, has_side_effects=True, vmem_limit_bytes=40 * 1024 * 1024
        ),
        cost_estimate=pl.CostEstimate(
            flops=2 * 6 * rows * 4 * INNER * INNER, bytes_accessed=6 << 20, transcendentals=0
        ),
    )(
        hbm(handoff),
        hbm(gate_input),
        hbm(source),
        hbm(long_filter),
        hbm(decay_rates),
        hbm(jnp.asarray(forward_table)),
        hbm(jnp.asarray(inverse_table)),
    )
    return pl.pallas_call(
        finish,
        out_shape=(
            jax.ShapeDtypeStruct(source.shape, BF16),
            jax.ShapeDtypeStruct(source.shape, BF16),
            jax.ShapeDtypeStruct(source.shape, F32),
        ),
        in_specs=[pl.BlockSpec(memory_space=pltpu.VMEM)] * 3,
        out_specs=[pl.BlockSpec(memory_space=pltpu.HBM)] * 3,
        scratch_shapes=[
            pltpu.VMEM(block, BF16),
            pltpu.VMEM(block, F32),
            pltpu.SemaphoreType.DMA((1 + 2 * (width // LANES),)),
        ],
        compiler_params=pltpu.CompilerParams(vmem_limit_bytes=4 * 1024 * 1024),
    )(*[pltpu.with_memory_space_constraint(r, pltpu.VMEM) for r in results])


def solution(mesh):
    tokens = P("pipe", "seq", None)
    return jax.shard_map(
        functools.partial(local, mesh.shape["seq"], mesh.shape["pipe"]),
        mesh=mesh,
        in_specs=(tokens, tokens, tokens, tokens, P("pipe", None)),
        out_specs=(tokens, tokens, tokens),
        check_vma=False,
    )
```

time: 27 us -> 26.1 us (0.967)
  Pallas kernels: 26.3 us -> 25.3 us
    pallas_call x1, Pallas kernels: 25.4 us -> 24.4 us  [local(): pl.pallas_call(functools.partial(kernel, n, nz), out_shape=(pltpu.VMEM(bl...]
where the time goes in v3:
time: 26.1 us; the launch traced here: 26 us
  Pallas kernels  25.3 us (97%)
  between operations  0.64 us (2%)
    pallas_call x1, Pallas kernels, local(): pl.pallas_call(functools.partial(kernel, n, nz), out_shape=(pltpu.VMEM(bl...  24.4 us
    pallas_call x1, Pallas kernels, local(): pl.pallas_call(finish, out_shape=(jax.ShapeDtypeStruct(source.shape, BF16...  0.92 us

profile of v3, /device:TPU:1, one launch (start us, length us, event | category | flops | bytes accessed | tf_op | source)
XLA Modules:
  0.0 26.0 jit_solution(6119090297027497854)
XLA Ops:
  0.6 24.4 %shard_map.94 = (bf16[128,512]{1,0:T(8,128)(2,1)S(1)}, bf16[32,2,16,128]{3,2,1,0:T(8,128)(2,1)S(1)}, f32[128,512]{1,0:T(8,128)S(1)}) custom-call(bf16[1,128,512]{2,1,0:T(8,128)(2,1)} %handoff.1, bf16[1,128,512]{2,1,0:T(8,128)(2,1)} %gate.1, bf16[1,128,512]{2,1,0:T(8,128)(2,1)} %source.1, bf16[1,128,512]{2,1,0:T(8,128)(2,1)} %filt.1, f32[1,512]{1,0:T(1,128)} %decay.1, ...), custom_call_target="tpu_custom_call" | custom-call | flops 1610612736 | bytes 6291456 | tf_op jit(solution)/shard_map/pallas_call | solution.py:365
  25.1 0.9 %shard_map.95 = (bf16[1,128,512]{2,1,0:T(8,128)(2,1)}, bf16[1,128,512]{2,1,0:T(8,128)(2,1)}, f32[1,128,512]{2,1,0:T(8,128)}) custom-call(bf16[128,512]{1,0:T(8,128)(2,1)S(1)} %get-tuple-element.6.gate_v, bf16[32,2,16,128]{3,2,1,0:T(8,128)(2,1)S(1)} %get-tuple-element.7.pair_v, f32[128,512]{1,0:T(8,128)S(1)} %get-tuple-element.8.mod_v), custom_call_target="tpu_custom_call" | custom-call | tf_op jit(solution)/shard_map/pallas_call | solution.py:410

commit v4 on v3

--- a/solution.py
+++ b/solution.py
@@ -64,6 +64,7 @@
     local_sem,
     pipe_ready,
     all_in,
+    zero_in,
     pipe_send,
     pipe_recv,
     send_sem,
@@ -103,23 +104,35 @@
     first, last = mz == 0, mz == nz - 1
     barrier = pltpu.get_barrier_semaphore()
 
-    @pl.when(jnp.logical_not(last))
-    def _():
-        pl.semaphore_signal(
-            barrier, inc=1, device_id={"pipe": above, "seq": second}, device_id_type=MESH
-        )
-
-    pl.semaphore_signal(barrier, inc=1, device_id={"seq": sibling}, device_id_type=MESH)
-    for dx, dy, dc in offsets:
-        if dc == 0:
-            at = xs[dx] * (ny * nc) + ys[dy] * nc
-            pl.semaphore_signal(barrier, inc=1, device_id={"seq": at}, device_id_type=MESH)
+    def greet(**place):
+        pl.semaphore_signal(barrier, inc=1, device_id=place, device_id_type=MESH)
 
     @pl.when(first)
     def _():
-        pl.semaphore_signal(
-            barrier, inc=1, device_id={"pipe": below, "seq": second}, device_id_type=MESH
-        )
+        greet(pipe=above, seq=second)
+
+        @pl.when(me == 0)
+        def _():
+            greet(seq=1)
+
+        @pl.when(me != 0)
+        def _():
+            for offset in offsets:
+                dest = index(offset)
+                pl.when(dest != 1)(functools.partial(greet, seq=dest))
+
+        greet(pipe=below, seq=second)
+
+    @pl.when(jnp.logical_not(first))
+    def _():
+        @pl.when(jnp.logical_not(last))
+        def _():
+            greet(pipe=above, seq=second)
+
+        greet(seq=sibling)
+        for dx, dy, dc in offsets:
+            if dc == 0:
+                greet(seq=xs[dx] * (ny * nc) + ys[dy] * nc)
 
     loads = [
         pltpu.make_async_copy(source.at[0], src_v, local_sem.at[0]),
@@ -147,14 +160,11 @@
         for q in range(chunks):
             pipe_copy(q).start()
 
-    @pl.when(core == 1)
-    def _():
-        pl.semaphore_wait(barrier, 1 + jnp.where(first, 0, 2) + jnp.where(last, 2, 0))
-
-        @pl.when(jnp.logical_not(first))
-        def _():
-            pl.semaphore_signal(pipe_ready, inc=1, device_id={"seq": sibling}, device_id_type=MESH)
-            pass_on()
+    @pl.when(jnp.logical_and(core == 1, jnp.logical_not(first)))
+    def _():
+        pl.semaphore_wait(barrier, 3 + jnp.where(last, 2, 0))
+        pl.semaphore_signal(pipe_ready, inc=1, device_id={"seq": sibling}, device_id_type=MESH)
+        pass_on()
 
         @pl.when(last)
         def _():
@@ -181,26 +191,45 @@
     send_first[:, 1] = by_channel(filt_v[...].astype(F32) * mod_v[...])
     recv_first[me] = send_first[me]
 
-    @pl.when(core == 0)
+    @pl.when(jnp.logical_and(first, me != 1))
+    def _():
+        pl.semaphore_wait(barrier, n - 1 - jnp.where(me == 0, 0, 1))
+
+        @pl.when(me == 2)
+        def _():
+            pl.semaphore_signal(all_in, inc=1, device_id={"seq": 1}, device_id_type=MESH)
+
+    @pl.when(jnp.logical_and(core == 0, jnp.logical_not(first)))
     def _():
         pl.semaphore_wait(barrier, n - 1)
+
+    @pl.when(jnp.logical_and(core == 0, jnp.logical_not(first)))
+    def _():
         pl.semaphore_signal(all_in, inc=1, device_id={"seq": sibling}, device_id_type=MESH)
 
-    @pl.when(core == 1)
+    @pl.when(jnp.logical_and(core == 1, jnp.logical_or(jnp.logical_not(first), me == 1)))
     def _():
         pl.semaphore_wait(all_in, 1)
+
+    def send(src, dst, sem, dest):
+        pltpu.make_async_remote_copy(
+            src_ref=src.at[dest],
+            dst_ref=dst.at[me],
+            send_sem=send_sem.at[sem],
+            recv_sem=recv_sem.at[sem],
+            device_id={"seq": dest},
+            device_id_type=MESH,
+        ).start()
 
     def exchange(src, dst, sem, places):
         for offset in places:
+            send(src, dst, sem, index(offset))
+
+    def exchange_early(src, dst, sem, places):
+        for offset in places:
             dest = index(offset)
-            pltpu.make_async_remote_copy(
-                src_ref=src.at[dest],
-                dst_ref=dst.at[me],
-                send_sem=send_sem.at[sem],
-                recv_sem=recv_sem.at[sem],
-                device_id={"seq": dest},
-                device_id_type=MESH,
-            ).start()
+            there = jnp.logical_or(jnp.logical_not(first), dest != 0)
+            pl.when(there)(functools.partial(send, src, dst, sem, dest))
 
     def whole(src, dst, sem):
         return pltpu.make_async_remote_copy(
@@ -212,7 +241,18 @@
             device_id_type=MESH,
         )
 
-    exchange(send_first, recv_first, 0, offsets)
+    exchange_early(send_first, recv_first, 0, offsets)
+
+    @pl.when(jnp.logical_and(first, me == 1))
+    def _():
+        pl.semaphore_wait(barrier, 1)
+        for offset in offsets:
+            dest = index(offset)
+
+            @pl.when(dest != 0)
+            def _():
+                pl.semaphore_signal(zero_in, inc=1, device_id={"seq": dest}, device_id_type=MESH)
+
 
     loads[3].wait()
     for q in range(chunks):
@@ -221,8 +261,17 @@
         cols = pl.ds(pl.multiple_of(chunk * LANES, LANES), LANES)
         product = grad_v[:, cols].astype(F32) * gate_v[:, cols].astype(F32)
         send_grad[pl.ds(chunk * per_chunk, per_chunk)] = by_channel(product.astype(BF16))
-        exchange(send_grad, recv_grad, 1, [o for o in offsets if o[0] == turns[q]])
+        exchange_early(send_grad, recv_grad, 1, [o for o in offsets if o[0] == turns[q]])
     recv_grad[me] = send_grad[me]
+
+    @pl.when(jnp.logical_and(first, me != 0))
+    def _():
+        @pl.when(me != 1)
+        def _():
+            pl.semaphore_wait(zero_in, 1)
+
+        send(send_first, recv_first, 0, 0)
+        send(send_grad, recv_grad, 1, 0)
 
     @pl.when(first)
     def _():
@@ -385,6 +434,7 @@
             pltpu.VMEM(one, BF16),
             pltpu.VMEM(two, BF16),
             pltpu.SemaphoreType.DMA((6,)),
+            pltpu.SemaphoreType.REGULAR,
             pltpu.SemaphoreType.REGULAR,
             pltpu.SemaphoreType.REGULAR,
             pltpu.SemaphoreType.DMA((width // LANES,)),

time: 26.1 us -> 25.8 us (0.989)
    pallas_call x1, Pallas kernels: 24.4 us -> 24.1 us  [local(): pl.pallas_call(functools.partial(kernel, n, nz), out_shape=(pltpu.VMEM(bl...]
where the time goes in v4:
time: 25.8 us; the launch traced here: 25.7 us
  Pallas kernels  25.1 us (97%)
  between operations  0.64 us (2%)
    pallas_call x1, Pallas kernels, local(): pl.pallas_call(functools.partial(kernel, n, nz), out_shape=(pltpu.VMEM(bl...  24.1 us
    pallas_call x1, Pallas kernels, local(): pl.pallas_call(finish, out_shape=(jax.ShapeDtypeStruct(source.shape, BF16...  0.92 us

profile of v4, /device:TPU:1, one launch (start us, length us, event | category | flops | bytes accessed | tf_op | source)
XLA Modules:
  0.0 25.7 jit_solution(18220736576776336230)
XLA Ops:
  0.6 24.1 %shard_map.94 = (bf16[128,512]{1,0:T(8,128)(2,1)S(1)}, bf16[32,2,16,128]{3,2,1,0:T(8,128)(2,1)S(1)}, f32[128,512]{1,0:T(8,128)S(1)}) custom-call(bf16[1,128,512]{2,1,0:T(8,128)(2,1)} %handoff.1, bf16[1,128,512]{2,1,0:T(8,128)(2,1)} %gate.1, bf16[1,128,512]{2,1,0:T(8,128)(2,1)} %source.1, bf16[1,128,512]{2,1,0:T(8,128)(2,1)} %filt.1, f32[1,512]{1,0:T(1,128)} %decay.1, ...), custom_call_target="tpu_custom_call" | custom-call | flops 1610612736 | bytes 6291456 | tf_op jit(solution)/shard_map/pallas_call | solution.py:414
  24.8 0.9 %shard_map.95 = (bf16[1,128,512]{2,1,0:T(8,128)(2,1)}, bf16[1,128,512]{2,1,0:T(8,128)(2,1)}, f32[1,128,512]{2,1,0:T(8,128)}) custom-call(bf16[128,512]{1,0:T(8,128)(2,1)S(1)} %get-tuple-element.6.gate_v, bf16[32,2,16,128]{3,2,1,0:T(8,128)(2,1)S(1)} %get-tuple-element.7.pair_v, f32[128,512]{1,0:T(8,128)S(1)} %get-tuple-element.8.mod_v), custom_call_target="tpu_custom_call" | custom-call | tf_op jit(solution)/shard_map/pallas_call | solution.py:460

commit v5 on v4

--- a/solution.py
+++ b/solution.py
@@ -98,42 +98,6 @@
     offsets = sorted(offsets, key=hops, reverse=True)[:-1]
     turns = sorted(range(nx), key=lambda d: min(d, nx - d), reverse=True)
 
-    core = lax.rem(me, nc)
-    second = me - core + 1
-    sibling = me + 1 - 2 * core
-    first, last = mz == 0, mz == nz - 1
-    barrier = pltpu.get_barrier_semaphore()
-
-    def greet(**place):
-        pl.semaphore_signal(barrier, inc=1, device_id=place, device_id_type=MESH)
-
-    @pl.when(first)
-    def _():
-        greet(pipe=above, seq=second)
-
-        @pl.when(me == 0)
-        def _():
-            greet(seq=1)
-
-        @pl.when(me != 0)
-        def _():
-            for offset in offsets:
-                dest = index(offset)
-                pl.when(dest != 1)(functools.partial(greet, seq=dest))
-
-        greet(pipe=below, seq=second)
-
-    @pl.when(jnp.logical_not(first))
-    def _():
-        @pl.when(jnp.logical_not(last))
-        def _():
-            greet(pipe=above, seq=second)
-
-        greet(seq=sibling)
-        for dx, dy, dc in offsets:
-            if dc == 0:
-                greet(seq=xs[dx] * (ny * nc) + ys[dy] * nc)
-
     loads = [
         pltpu.make_async_copy(source.at[0], src_v, local_sem.at[0]),
         pltpu.make_async_copy(filt.at[0], filt_v, local_sem.at[1]),
@@ -144,6 +108,42 @@
     ]
     for load in loads:
         load.start()
+
+    core = lax.rem(me, nc)
+    second = me - core + 1
+    sibling = me + 1 - 2 * core
+    first, last = mz == 0, mz == nz - 1
+    barrier = pltpu.get_barrier_semaphore()
+
+    def greet(**place):
+        pl.semaphore_signal(barrier, inc=1, device_id=place, device_id_type=MESH)
+
+    @pl.when(first)
+    def _():
+        greet(pipe=above, seq=second)
+
+        @pl.when(me == 0)
+        def _():
+            greet(seq=1)
+
+        @pl.when(me != 0)
+        def _():
+            for offset in offsets:
+                dest = index(offset)
+                pl.when(dest != 1)(functools.partial(greet, seq=dest))
+
+        greet(pipe=below, seq=second)
+
+    @pl.when(jnp.logical_not(first))
+    def _():
+        @pl.when(jnp.logical_not(last))
+        def _():
+            greet(pipe=above, seq=second)
+
+        greet(seq=sibling)
+        for dx, dy, dc in offsets:
+            if dc == 0:
+                greet(seq=xs[dx] * (ny * nc) + ys[dy] * nc)
 
     def pipe_copy(q):
         at = pl.multiple_of(xs[turns[q]] * LANES, LANES)
@@ -308,17 +308,21 @@
                 right = [
                     (spec[other, part[b], real], spec[other, part[b], imag]) for b in range(blocks)
                 ]
+                mixed = [kr - ki if correlate else kr + ki for kr, ki in fold]
+                sums = [br + bi for br, bi in right]
                 for i in range(blocks):
-                    total_r = total_i = None
+                    real_sum = imag_sum = mixed_sum = None
                     for j in range(i, blocks) if correlate else range(i + 1):
-                        kr, ki = fold[j - i] if correlate else fold[i - j]
-                        br, bi = right[j]
-                        if correlate:
-                            term_r, term_i = kr * br + ki * bi, kr * bi - ki * br
-                        else:
-                            term_r, term_i = kr * br - ki * bi, kr * bi + ki * br
-                        total_r = term_r if total_r is None else total_r + term_r
-                        total_i = term_i if total_i is None else total_i + term_i
+                        d = j - i if correlate else i - j
+                        reals, imags = fold[d][0] * right[j][0], fold[d][1] * right[j][1]
+                        mixes = mixed[d] * sums[j]
+                        real_sum = reals if real_sum is None else real_sum + reals
+                        imag_sum = imags if imag_sum is None else imag_sum + imags
+                        mixed_sum = mixes if mixed_sum is None else mixed_sum + mixes
+                    if correlate:
+                        total_r, total_i = real_sum + imag_sum, mixed_sum - real_sum + imag_sum
+                    else:
+                        total_r, total_i = real_sum - imag_sum, mixed_sum - real_sum - imag_sum
                     to = pl.ds(base + i * chans + half, 8)
                     prod[to, real] = total_r
                     prod[to, imag] = total_i

time: 25.8 us -> 25.7 us (level)
  no operation moved by 1% of the time
where the time goes in v5:
time: 25.7 us; the launch traced here: 25.5 us
  Pallas kernels  24.9 us (97%)
  between operations  0.64 us (2%)
    pallas_call x1, Pallas kernels, local(): pl.pallas_call(functools.partial(kernel, n, nz), out_shape=(pltpu.VMEM(bl...  24 us
    pallas_call x1, Pallas kernels, local(): pl.pallas_call(finish, out_shape=(jax.ShapeDtypeStruct(source.shape, BF16...  0.92 us

profile of v5, /device:TPU:1, one launch (start us, length us, event | category | flops | bytes accessed | tf_op | source)
XLA Modules:
  0.0 25.5 jit_solution(7062625844770229052)
XLA Ops:
  0.6 24.0 %shard_map.94 = (bf16[128,512]{1,0:T(8,128)(2,1)S(1)}, bf16[32,2,16,128]{3,2,1,0:T(8,128)(2,1)S(1)}, f32[128,512]{1,0:T(8,128)S(1)}) custom-call(bf16[1,128,512]{2,1,0:T(8,128)(2,1)} %handoff.1, bf16[1,128,512]{2,1,0:T(8,128)(2,1)} %gate.1, bf16[1,128,512]{2,1,0:T(8,128)(2,1)} %source.1, bf16[1,128,512]{2,1,0:T(8,128)(2,1)} %filt.1, f32[1,512]{1,0:T(1,128)} %decay.1, ...), custom_call_target="tpu_custom_call" | custom-call | flops 1610612736 | bytes 6291456 | tf_op jit(solution)/shard_map/pallas_call | solution.py:418
  24.6 0.9 %shard_map.95 = (bf16[1,128,512]{2,1,0:T(8,128)(2,1)}, bf16[1,128,512]{2,1,0:T(8,128)(2,1)}, f32[1,128,512]{2,1,0:T(8,128)}) custom-call(bf16[128,512]{1,0:T(8,128)(2,1)S(1)} %get-tuple-element.6.gate_v, bf16[32,2,16,128]{3,2,1,0:T(8,128)(2,1)S(1)} %get-tuple-element.7.pair_v, f32[128,512]{1,0:T(8,128)S(1)} %get-tuple-element.8.mod_v), custom_call_target="tpu_custom_call" | custom-call | tf_op jit(solution)/shard_map/pallas_call | solution.py:464
